TPU v7x, 32 devices: a whole 2x2x4 slice. The times are simulated.
32 devices in a mesh: grp: 4 (over y, x), dev: 8 (over z, core).
Axes of the slice: x: 2, y: 2, z: 4, core: 2. Of those that a mesh axis runs over, the one named last changes fastest.
Arguments:
- block_vectors: float32 [16384, 64], P(('grp', 'dev')), may hold values from -6 to 6
- hamiltonian: float32 [256, 64, 2048], P(('grp', 'dev')), may hold values from -0.125 to 0.125
- pattern: int32 [256, 32], P(('grp', 'dev')), may hold values from 0 to 255, as said below
- owned_blocks: int32 [32], P(('grp', 'dev')), may hold values from 1 to 8, as said below
- spectrum: float32 [2], replicated, may hold values from 0.5 to 2
Outputs:
- basis: float32 [16384, 64], P(('grp', 'dev'))
- r_factor: float32 [64, 64], replicated
Inputs may be any that keep to these rules, and one draw needn't show every extreme that they name: pattern[b, 0] = b; every other entry is b + o clipped to the slots, for a distinct nonzero o with |o| <= 16. `owned_blocks`: some device owns all 8 slots.
All inputs are finite; a program needn't handle non-finite values.
Results may differ from a plain program's by a relative error of at most 0.0003.
Values sent between devices are 32-bit elements; how exact they have to be, the bound alone decides.
No kernel may reach another device: no remote copies, remote signals or barrier semaphores. Data moves between devices by JAX's collectives and lax.ppermute only.
A program may use at most 64 MiB of HBM per device.

v0:
```python
import jax
import jax.numpy as jnp
from jax import lax
from jax.sharding import PartitionSpec as P

BAND = 16


def shifted(block, axis, distance):
    devices = range(lax.axis_size(axis))
    route = [(i - distance, i) for i in devices if i - distance in devices]
    return lax.ppermute(block, axis, route)


def send_direct(values, distance):
    return shifted(values, ("grp", "dev"), distance)


def extend_band(values, reach_dev):
    lowers = []
    uppers = []
    for distance in range(reach_dev, 0, -1):
        lowers.append(send_direct(values, distance))
    for distance in range(1, reach_dev + 1):
        uppers.append(send_direct(values, -distance))
    return jnp.concatenate(lowers + [values] + uppers, axis=0)


def apply_matrix(values, hamiltonian, local_index, reach_dev):
    extended = extend_band(values, reach_dev)
    block_count, neighbours = local_index.shape
    picked = jnp.take(extended, local_index, axis=0)
    picked = picked.reshape(block_count, neighbours * values.shape[1], values.shape[2])
    return jnp.einsum("gik,gkc->gic", hamiltonian, picked, precision=lax.Precision.HIGHEST)


def summed_gram(flat):
    local_gram = jnp.dot(
        flat.T, flat, precision=lax.Precision.HIGHEST, preferred_element_type=jnp.float32
    )
    return lax.psum(local_gram, ("grp", "dev"))


def cholesky_step(flat):
    gram_total = summed_gram(flat)
    upper = jnp.linalg.cholesky(gram_total).T
    ortho = jax.scipy.linalg.solve_triangular(upper.T, flat.T, lower=True).T
    return (ortho, upper)


def on_device(block_vectors, hamiltonian, pattern, owned_blocks, spectrum):
    block_count = pattern.shape[0]
    block_size = hamiltonian.shape[1]
    columns = block_vectors.shape[1]
    reach_dev = (BAND + block_count - 1) // block_count
    first_block = lax.axis_index(("grp", "dev")) * block_count
    local_index = pattern - first_block + reach_dev * block_count
    live_mask = (jnp.arange(block_count, dtype=jnp.int32) < owned_blocks[0]).astype(jnp.float32)[
        :, None, None
    ]
    shift_value = spectrum[0]
    scale_value = spectrum[1]
    first_vec = block_vectors.reshape(block_count, block_size, columns) * live_mask
    second_vec = live_mask * (
        (apply_matrix(first_vec, hamiltonian, local_index, reach_dev) - shift_value * first_vec)
        / scale_value
    )
    third_vec = live_mask * (
        2.0
        * (apply_matrix(second_vec, hamiltonian, local_index, reach_dev) - shift_value * second_vec)
        / scale_value
        - first_vec
    )
    flat = third_vec.reshape(block_count * block_size, columns)
    ortho_one, upper_one = cholesky_step(flat)
    ortho_two, upper_two = cholesky_step(ortho_one)
    upper_all = jnp.dot(
        upper_two, upper_one, precision=lax.Precision.HIGHEST, preferred_element_type=jnp.float32
    )
    total = jnp.sqrt(
        jnp.float32(block_count * block_size * lax.axis_size("grp") * lax.axis_size("dev"))
    )
    return (ortho_two * total, upper_all / total)


def solution(mesh):
    placed = (
        P(("grp", "dev"), None),
        P(("grp", "dev"), None, None),
        P(("grp", "dev"), None),
        P(("grp", "dev")),
        P(),
    )
    return jax.shard_map(
        on_device,
        mesh=mesh,
        in_specs=placed,
        out_specs=(P(("grp", "dev"), None), P()),
        check_vma=False,
    )
```

profile of v0, /device:TPU:0, one launch (start us, length us, event | category | flops | bytes accessed | tf_op | source)
XLA Modules:
  0.0 225.4 jit_solution(5795718973139999326)
XLA Ops:
  1.3 1.0 reshape.34
  2.3 0.1 copy_multiply_fusion
  2.4 1.3 collective-permute-start.3
  3.7 1.3 collective-permute-start.2
  5.0 3.0 %collective-permute-start.1 = (f32[8,64,64]{1,2,0:T(8,128)S(1)}, f32[8,64,64]{1,2,0:T(8,128)S(1)}, u32[]{:S(2)}, u32[]{:S(2)}) collective-permute-start(f32[8,64,64]{1,2,0:T(8,128)S(1)} %copy_multiply_fusion), channel_id=1, source_target_pairs={{0,1},{1,2},{2,3},{3,4},{4,5},{5,6},{6,7},{7,8},{8,9},{9,10},{10,1... | collective-permute-start | bytes 393224 | tf_op jit(solution)/shard_map/ppermute | solution.py:12
  8.0 5.6 %collective-permute-start = (f32[8,64,64]{1,2,0:T(8,128)S(1)}, f32[8,64,64]{1,2,0:T(8,128)S(1)}, u32[]{:S(2)}, u32[]{:S(2)}) collective-permute-start(f32[8,64,64]{1,2,0:T(8,128)S(1)} %copy_multiply_fusion), channel_id=1, source_target_pairs={{0,2},{1,3},{2,4},{3,5},{4,6},{5,7},{6,8},{7,9},{8,10},{9,11},{10,... | collective-permute-start | bytes 393224 | tf_op jit(solution)/shard_map/ppermute | solution.py:12
  13.6 0.7 compare_and_fusion
  14.3 1.3 fusion.29
  15.6 0.1 reshape.58
  15.7 3.9 %collective-permute-done = f32[8,64,64]{1,2,0:T(8,128)S(1)} collective-permute-done((f32[8,64,64]{1,2,0:T(8,128)S(1)}, f32[8,64,64]{1,2,0:T(8,128)S(1)}, u32[]{:S(2)}, u32[]{:S(2)}) %collective-permute-start) | collective-permute-done | bytes 131104 | tf_op jit(solution)/shard_map/ppermute | solution.py:12
  19.7 0.0 collective-permute-done.1
  19.7 0.1 constant_dynamic-update-slice_fusion.2
  19.8 0.0 collective-permute-done.2
  19.9 0.0 collective-permute-done.3
  19.9 4.4 %gather_fusion = f32[256,64,64]{1,2,0:T(8,128)} fusion(f32[40,64,64]{1,2,0:T(8,128)S(1)} %constant_dynamic-update-slice_fusion, s32[1024]{0:T(1024)S(1)} %pad_clamp_fusion), kind=kCustom, calls=%fused_computation.clone | custom fusion | bytes 8389632 | tf_op jit(solution)/shard_map/jit(_take)/gather | solution.py:32
  24.3 3.8 %broadcast_select_fusion.1 = f32[8,32,64,64]{2,3,1,0:T(8,128)S(1)} fusion(f32[8,32,64,64]{2,3,1,0:T(8,128)} %bitcast.73, pred[8,32]{1,0:T(8,128)(4,1)S(1)} %get-tuple-element.4), kind=kLoop, calls=%fused_computation.3 | loop fusion | flops 1048576 | bytes 8388864 | tf_op jit(solution)/shard_map/jit(_take)/select_n | solution.py:32
  28.1 8.0 %copy.15 = f32[8,32,64,64]{2,1,3,0:T(8,128)} copy(f32[8,32,64,64]{2,3,1,0:T(8,128)S(1)} %broadcast_select_fusion.1) | data formatting | bytes 8388608 | tf_op jit(solution)/shard_map/jit(_take)/select_n | solution.py:32
  36.1 7.8 %reshape.35 = f32[8,2048,64]{1,2,0:T(8,128)} reshape(f32[8,32,64,64]{2,1,3,0:T(8,128)} %copy.15) | data formatting | bytes 8388608 | tf_op jit(solution)/shard_map/reshape | solution.py:33
  43.9 8.7 %fusion.4 = f32[8,64,64]{1,2,0:T(8,128)S(1)} fusion(f32[8,2048,64]{1,2,0:T(8,128)} %reshape.35, f32[8,64,2048]{2,1,0:T(8,128)} %param.11, f32[]{:T(128)} %bitcast.4, f32[]{:T(128)} %bitcast.3, f32[8]{0:T(128)S(1)} %compare_convert_fusion, f32[8,64,64]{1,0,2:T(8,128)S(1)} %reshape.34), kind=kOutput, calls=%fused_computation.10 | convolution fusion | flops 805470208 | bytes 8650792 | tf_op jit(solution)/shard_map/gik,gkc->gic/dot_general | solution.py:34
  52.6 4.4 %collective-permute-start.4 = (f32[8,64,64]{1,2,0:T(8,128)S(1)}, f32[8,64,64]{1,2,0:T(8,128)S(1)}, u32[]{:S(2)}, u32[]{:S(2)}) collective-permute-start(f32[8,64,64]{1,2,0:T(8,128)S(1)} %fusion.4), channel_id=1, source_target_pairs={{0,2},{1,3},{2,4},{3,5},{4,6},{5,7},{6,8},{7,9},{8,10},{9,11},{10,... | collective-permute-start | bytes 393224 | tf_op jit(solution)/shard_map/ppermute | solution.py:12
  57.0 2.1 collective-permute-start.5
  59.1 1.3 collective-permute-start.7
  60.4 1.5 collective-permute-start.6
  61.9 1.7 collective-permute-done.4
  63.6 0.0 collective-permute-done.5
  63.7 2.0 collective-permute-done.6
  65.7 8.9 %collective-permute-done.7 = f32[8,64,64]{1,2,0:T(8,128)S(1)} collective-permute-done((f32[8,64,64]{1,2,0:T(8,128)S(1)}, f32[8,64,64]{1,2,0:T(8,128)S(1)}, u32[]{:S(2)}, u32[]{:S(2)}) %collective-permute-start.7) | collective-permute-done | bytes 131104 | tf_op jit(solution)/shard_map/ppermute | solution.py:12
  74.6 4.4 %gather_fusion.1 = f32[256,64,64]{1,2,0:T(8,128)} fusion(f32[40,64,64]{1,2,0:T(8,128)S(1)} %constant_dynamic-update-slice_fusion.5, s32[1024]{0:T(1024)S(1)} %pad_clamp_fusion), kind=kCustom, calls=%fused_computation.1.clone | custom fusion | bytes 8389632 | tf_op jit(solution)/shard_map/jit(_take)/gather | solution.py:32
  78.9 3.8 %broadcast_select_fusion = f32[8,32,64,64]{2,3,1,0:T(8,128)S(1)} fusion(f32[8,32,64,64]{2,3,1,0:T(8,128)} %bitcast.72, pred[8,32]{1,0:T(8,128)(4,1)S(1)} %get-tuple-element.4), kind=kLoop, calls=%fused_computation.2 | loop fusion | flops 1048576 | bytes 8388864 | tf_op jit(solution)/shard_map/jit(_take)/select_n | solution.py:32
  82.8 8.0 %copy.16 = f32[8,32,64,64]{2,1,3,0:T(8,128)} copy(f32[8,32,64,64]{2,3,1,0:T(8,128)S(1)} %broadcast_select_fusion) | data formatting | bytes 8388608 | tf_op jit(solution)/shard_map/jit(_take)/select_n | solution.py:32
  90.8 7.8 %reshape.36 = f32[8,2048,64]{1,2,0:T(8,128)} reshape(f32[8,32,64,64]{2,1,3,0:T(8,128)} %copy.16) | data formatting | bytes 8388608 | tf_op jit(solution)/shard_map/reshape | solution.py:33
  98.6 8.7 %fusion.7 = f32[8,64,64]{1,2,0:T(8,128)S(1)} fusion(f32[8,2048,64]{1,2,0:T(8,128)} %reshape.36, f32[8,64,2048]{2,1,0:T(8,128)} %param.11, f32[8,64,64]{1,2,0:T(8,128)S(1)} %fusion.4, f32[]{:T(128)} %bitcast.4, f32[]{:T(128)} %bitcast.3, f32[8]{0:T(128)S(1)} %compare_convert_fusion, f32[8,64,64]{1,0,2:T(8,128)S(1)} %reshape.34), kind=kOutput, calls=%fused_computation.13 | convolution fusion | flops 805535744 | bytes 8781864 | tf_op jit(solution)/shard_map/gik,gkc->gic/dot_general | solution.py:34
  107.3 0.4 convolution_bitcast_fusion.2
  107.7 0.2 copy.20
  107.8 49.4 %psum.14 = f32[64,64]{0,1:T(8,128)S(1)} all-reduce(f32[64,64]{0,1:T(8,128)S(1)} %convolution_bitcast_fusion.2), channel_id=1, replica_groups=mesh['grp'=4,'dev'=8] {'grp','dev'}, use_global_device_ids=true, to_apply=%region_0.0 | all-reduce | flops 4096 | bytes 32768 | tf_op jit(solution)/shard_map/psum | solution.py:41
  157.3 0.1 reshape.37
  157.4 0.1 copy.19
  157.5 5.8 %cholesky.44 = f32[64,64]{1,0:T(8,128)S(1)} custom-call(f32[64,64]{1,0:T(8,128)S(1)} %fusion.14), custom_call_target="Cholesky" | custom-call | tf_op jit(solution)/shard_map/jit(cholesky)/cholesky | solution.py:46
  163.3 0.6 compare_reduce_fusion.1
  164.0 0.7 fusion.18
  164.7 4.9 %custom-call.6 = f32[1,64,64]{1,2,0:T(8,128)S(1)} custom-call(f32[1,64,64]{2,1,0:T(8,128)S(1)} %fusion.18), custom_call_target="InvertDiagBlocksLowerTriangular" | custom-call | tf_op jit(solution)/shard_map/jit(_solve_triangular)/triangular_solve | solution.py:47
  169.5 0.3 fusion.9
  169.9 0.3 fusion.30
  170.2 39.7 %psum.15 = f32[64,64]{0,1:T(8,128)S(1)} all-reduce(f32[64,64]{0,1:T(8,128)S(1)} %fusion.30), channel_id=1, replica_groups=mesh['grp'=4,'dev'=8] {'grp','dev'}, use_global_device_ids=true, to_apply=%region_3.7 | all-reduce | flops 4096 | bytes 32768 | tf_op jit(solution)/shard_map/psum | solution.py:41
  209.9 0.1 copy.22
  210.0 5.8 %cholesky.55 = f32[64,64]{1,0:T(8,128)S(1)} custom-call(f32[64,64]{1,0:T(8,128)S(1)} %fusion.12), custom_call_target="Cholesky" | custom-call | tf_op jit(solution)/shard_map/jit(cholesky)/cholesky | solution.py:46
  215.8 0.7 compare_reduce_fusion
  216.6 2.2 convolution_multiply_fusion.1
  218.8 0.7 select_bitcast_fusion
  219.5 4.9 %custom-call.7 = f32[1,64,64]{1,2,0:T(8,128)S(1)} custom-call(f32[1,64,64]{2,1,0:T(8,128)S(1)} %select_bitcast_fusion), custom_call_target="InvertDiagBlocksLowerTriangular" | custom-call | tf_op jit(solution)/shard_map/jit(_solve_triangular)/triangular_solve | solution.py:47
  224.4 1.0 fusion.8
  (15 shorter events, 0.3 us)
Async XLA Ops:
  2.4 17.5 %collective-permute-start.3 = (f32[8,64,64]{1,2,0:T(8,128)S(1)}, f32[8,64,64]{1,2,0:T(8,128)S(1)}, u32[]{:S(2)}, u32[]{:S(2)}) collective-permute-start(f32[8,64,64]{1,2,0:T(8,128)S(1)} %copy_multiply_fusion), channel_id=1, source_target_pairs={{2,0},{3,1},{4,2},{5,3},{6,4},{7,5},{8,6},{9,7},{10,8},{11,9},{12,... | collective-permute-start | bytes 393224 | tf_op jit(solution)/shard_map/ppermute | solution.py:12
  3.7 16.1 %collective-permute-start.2 = (f32[8,64,64]{1,2,0:T(8,128)S(1)}, f32[8,64,64]{1,2,0:T(8,128)S(1)}, u32[]{:S(2)}, u32[]{:S(2)}) collective-permute-start(f32[8,64,64]{1,2,0:T(8,128)S(1)} %copy_multiply_fusion), channel_id=1, source_target_pairs={{1,0},{2,1},{3,2},{4,3},{5,4},{6,5},{7,6},{8,7},{9,8},{10,9},{11,1... | collective-permute-start | bytes 393224 | tf_op jit(solution)/shard_map/ppermute | solution.py:12
  5.0 14.7 %collective-permute-start.1 = (f32[8,64,64]{1,2,0:T(8,128)S(1)}, f32[8,64,64]{1,2,0:T(8,128)S(1)}, u32[]{:S(2)}, u32[]{:S(2)}) collective-permute-start(f32[8,64,64]{1,2,0:T(8,128)S(1)} %copy_multiply_fusion), channel_id=1, source_target_pairs={{0,1},{1,2},{2,3},{3,4},{4,5},{5,6},{6,7},{7,8},{8,9},{9,10},{10,1... | collective-permute-start | bytes 393224 | tf_op jit(solution)/shard_map/ppermute | solution.py:12
  8.0 11.6 %collective-permute-start = (f32[8,64,64]{1,2,0:T(8,128)S(1)}, f32[8,64,64]{1,2,0:T(8,128)S(1)}, u32[]{:S(2)}, u32[]{:S(2)}) collective-permute-start(f32[8,64,64]{1,2,0:T(8,128)S(1)} %copy_multiply_fusion), channel_id=1, source_target_pairs={{0,2},{1,3},{2,4},{3,5},{4,6},{5,7},{6,8},{7,9},{8,10},{9,11},{10,... | collective-permute-start | bytes 393224 | tf_op jit(solution)/shard_map/ppermute | solution.py:12
  52.6 11.0 %collective-permute-start.4 = (f32[8,64,64]{1,2,0:T(8,128)S(1)}, f32[8,64,64]{1,2,0:T(8,128)S(1)}, u32[]{:S(2)}, u32[]{:S(2)}) collective-permute-start(f32[8,64,64]{1,2,0:T(8,128)S(1)} %fusion.4), channel_id=1, source_target_pairs={{0,2},{1,3},{2,4},{3,5},{4,6},{5,7},{6,8},{7,9},{8,10},{9,11},{10,... | collective-permute-start | bytes 393224 | tf_op jit(solution)/shard_map/ppermute | solution.py:12
  57.0 6.6 %collective-permute-start.5 = (f32[8,64,64]{1,2,0:T(8,128)S(1)}, f32[8,64,64]{1,2,0:T(8,128)S(1)}, u32[]{:S(2)}, u32[]{:S(2)}) collective-permute-start(f32[8,64,64]{1,2,0:T(8,128)S(1)} %fusion.4), channel_id=1, source_target_pairs={{0,1},{1,2},{2,3},{3,4},{4,5},{5,6},{6,7},{7,8},{8,9},{9,10},{10,1... | collective-permute-start | bytes 393224 | tf_op jit(solution)/shard_map/ppermute | solution.py:12
  59.1 15.5 %collective-permute-start.7 = (f32[8,64,64]{1,2,0:T(8,128)S(1)}, f32[8,64,64]{1,2,0:T(8,128)S(1)}, u32[]{:S(2)}, u32[]{:S(2)}) collective-permute-start(f32[8,64,64]{1,2,0:T(8,128)S(1)} %fusion.4), channel_id=1, source_target_pairs={{2,0},{3,1},{4,2},{5,3},{6,4},{7,5},{8,6},{9,7},{10,8},{11,9},{12,... | collective-permute-start | bytes 393224 | tf_op jit(solution)/shard_map/ppermute | solution.py:12
  60.4 5.3 %collective-permute-start.6 = (f32[8,64,64]{1,2,0:T(8,128)S(1)}, f32[8,64,64]{1,2,0:T(8,128)S(1)}, u32[]{:S(2)}, u32[]{:S(2)}) collective-permute-start(f32[8,64,64]{1,2,0:T(8,128)S(1)} %fusion.4), channel_id=1, source_target_pairs={{1,0},{2,1},{3,2},{4,3},{5,4},{6,5},{7,6},{8,7},{9,8},{10,9},{11,1... | collective-permute-start | bytes 393224 | tf_op jit(solution)/shard_map/ppermute | solution.py:12
where the time goes:
time: 226 us; the launch traced here: 225 us
  blocking collectives  89.1 us (39%)
  local copies, waits for them, and re-layouts  43.3 us (19%)
  other arithmetic  32.9 us (15%)
  matrix products  21.5 us (10%)
  starting transfers between devices  20.4 us (9%)
  waiting for transfers between devices  16.5 us (7%)
    psum x2, blocking collectives, summed_gram(): return lax.psum(local_gram, ('grp', 'dev'))  89.1 us
    ppermute x8, starting transfers between devices, shifted(): return lax.ppermute(block, axis, route)  20.4 us
    dot_general x2, matrix products, apply_matrix(): jnp.einsum('gik,gkc->gic', hamiltonian, picked, precision=lax.Precision.H...  17.4 us
    ppermute x8, waiting for transfers between devices, shifted(): return lax.ppermute(block, axis, route)  16.5 us
    select_n x2, local copies, waits for them, and re-layouts, apply_matrix(): picked = jnp.take(extended, local_index, axis=0)  16 us
    reshape x2, local copies, waits for them, and re-layouts, apply_matrix(): picked.reshape(block_count, neighbours * values.shape[1], values.shape[2])  15.6 us
    another operation x6, other arithmetic, cholesky_step(): upper = jnp.linalg.cholesky(gram_total).T  13.1 us
    another operation x4, other arithmetic, cholesky_step(): ortho = jax.scipy.linalg.solve_triangular(upper.T, flat.T, lower=True).T  11.1 us
  transfers between devices with their start and end apart: 8, of which 4 were waited for; matrix products, arithmetic and copies ran while one was open for 1% of the time, Pallas kernels for 0%

commit v1 on v0

v1 whole, which is shorter than its diff:
```python
import functools

import jax
import jax.numpy as jnp
from jax import lax
from jax.experimental import pallas as pl
from jax.experimental.pallas import tpu as pltpu
from jax.sharding import PartitionSpec as P

BAND = 16
AXES = ("grp", "dev")
SPLITS = 3


def shifted(block, distance):
    devices = range(lax.axis_size(AXES))
    route = [(i - distance, i) for i in devices if i - distance in devices]
    return lax.ppermute(block, AXES, route)


def split_float(values):
    parts = []
    rest = values
    for _ in range(SPLITS - 1):
        part = rest.astype(jnp.bfloat16)
        parts.append(part)
        rest = rest - part.astype(jnp.float32)
    parts.append(rest.astype(jnp.bfloat16))
    return jnp.concatenate(parts, axis=0)


def joined_product(product, rows, columns):
    def part(i, j):
        return product[i * rows : (i + 1) * rows, j * columns : (j + 1) * columns]

    second = part(0, 2) + part(1, 1) + part(2, 0)
    first = part(0, 1) + part(1, 0)
    return part(0, 0) + (first + second)


def apply_kernel(
    first_apply,
    reach_dev,
    pattern_ref,
    owned_ref,
    spectrum_ref,
    *refs,
):
    sources = refs[: 2 * reach_dev + 1]
    refs = refs[2 * reach_dev + 1 :]
    if first_apply:
        matrix_ref, out_ref, held, window, product, arrived = refs
    else:
        start_ref, matrix_ref, out_ref, gram_ref, held, window, product, arrived = refs
    own_ref = sources[reach_dev]
    columns, rows = own_ref.shape
    block_count, block_size, width = held.shape
    neighbours = width // block_size

    def fetch(b):
        return pltpu.make_async_copy(matrix_ref.at[b], held.at[b], arrived.at[b])

    for b in range(block_count):
        fetch(b).start()
    for s, source in enumerate(sources):
        window[s * rows : (s + 1) * rows, :] = split_float(source[...]).T

    first_slot = reach_dev * block_count - pattern_ref[0, 0]
    chunk = 4
    for b in range(block_count):
        fetch(b).wait()
        total = None
        for c in range(0, neighbours, chunk):
            left = split_float(held[b, :, c * block_size : (c + chunk) * block_size])
            picked = []
            for k in range(c, c + chunk):
                slot = pattern_ref[b, k] + first_slot
                start = pl.multiple_of(slot * block_size, block_size)
                picked.append(window[pl.ds(start, block_size), :])
            right = jnp.concatenate(picked, axis=0)
            term = jnp.dot(left, right, preferred_element_type=jnp.float32)
            total = term if total is None else total + term
        product[b * block_size : (b + 1) * block_size, :] = joined_product(
            total, block_size, columns
        )

    live_rows = owned_ref[0] * block_size
    live = lax.broadcasted_iota(jnp.int32, (columns, rows), 1) < live_rows
    shift_value = spectrum_ref[0]
    scale_value = spectrum_ref[1]
    moved = product[...].T - shift_value * own_ref[...]
    if first_apply:
        out_ref[...] = jnp.where(live, moved / scale_value, 0.0)
    else:
        result = jnp.where(live, 2.0 * moved / scale_value - start_ref[...], 0.0)
        out_ref[...] = result
        parts = split_float(result)
        gram = lax.dot_general(
            parts, parts, (((1,), (1,)), ((), ())), preferred_element_type=jnp.float32
        )
        gram_ref[...] = joined_product(gram, columns, columns)


def apply_matrix(pattern, owned_blocks, spectrum, sources, start, hamiltonian):
    columns, rows = sources[0].shape
    block_count, block_size, width = hamiltonian.shape
    reach_dev = len(sources) // 2
    first_apply = start is None
    scalar = pl.BlockSpec(memory_space=pltpu.SMEM)
    vector = pl.BlockSpec(memory_space=pltpu.VMEM)
    far = pl.BlockSpec(memory_space=pl.ANY)
    out = jax.ShapeDtypeStruct((columns, rows), jnp.float32)
    gram = jax.ShapeDtypeStruct((columns, columns), jnp.float32)
    operands = list(sources) + ([] if first_apply else [start])
    return pl.pallas_call(
        functools.partial(apply_kernel, first_apply, reach_dev),
        out_shape=out if first_apply else (out, gram),
        in_specs=[scalar] * 3 + [vector] * len(operands) + [far],
        out_specs=vector if first_apply else (vector, vector),
        scratch_shapes=[
            pltpu.VMEM((block_count, block_size, width), jnp.float32),
            pltpu.VMEM((len(sources) * rows, SPLITS * columns), jnp.bfloat16),
            pltpu.VMEM((rows, columns), jnp.float32),
            pltpu.SemaphoreType.DMA((block_count,)),
        ],
        compiler_params=pltpu.CompilerParams(vmem_limit_bytes=32 * 2**20),
        name="apply_first" if first_apply else "apply_second",
    )(pattern, owned_blocks, spectrum, *operands, hamiltonian)


def factor_kernel(total, gram_ref, flat_ref, basis_ref, upper_ref, spread_ref):
    columns = gram_ref.shape[0]
    tile = 8
    width = 2 * columns
    gram = gram_ref[...]
    row = lax.broadcasted_iota(jnp.int32, (columns, columns), 0)
    lane = lax.broadcasted_iota(jnp.int32, (columns, columns), 1)
    unit = (row == lane).astype(jnp.float32)
    whole = jnp.concatenate([gram, unit], axis=1)
    tiles = [whole[i * tile : (i + 1) * tile, :] for i in range(columns // tile)]
    place = lax.broadcasted_iota(jnp.int32, (tile, width), 0)
    for j in range(columns):
        home, inner = divmod(j, tile)
        pivot_row = tiles[home][inner : inner + 1, :]
        scaled = pivot_row / pivot_row[:, j : j + 1]
        for i in range(home, columns // tile):
            factor = jnp.broadcast_to(tiles[i][:, j : j + 1], (tile, width))
            if i == home:
                factor = jnp.where(place > inner, factor, 0.0)
            tiles[i] = tiles[i] - factor * scaled
    done = jnp.concatenate(tiles, axis=0)
    weighted = done[:, :columns]
    diagonal = jnp.sum(jnp.where(row == lane, weighted, 0.0), axis=1, keepdims=True)
    root = jnp.sqrt(diagonal)
    upper = jnp.where(row <= lane, weighted / root, 0.0)
    inverse = done[:, columns:] / root
    upper_ref[...] = upper / total
    size = jnp.sum(jnp.where(row == lane, gram, 0.0), axis=0, keepdims=True)
    spread_ref[...] = jnp.broadcast_to(jnp.sum(inverse * inverse * size), spread_ref.shape)
    ortho = jnp.dot(
        inverse,
        flat_ref[...],
        precision=lax.Precision.HIGHEST,
        preferred_element_type=jnp.float32,
    )
    basis_ref[...] = ortho * total


def factor(gram, flat, total):
    vector = pl.BlockSpec(memory_space=pltpu.VMEM)
    return pl.pallas_call(
        functools.partial(factor_kernel, total),
        out_shape=(
            jax.ShapeDtypeStruct(flat.shape, jnp.float32),
            jax.ShapeDtypeStruct(gram.shape, jnp.float32),
            jax.ShapeDtypeStruct((8, 128), jnp.float32),
        ),
        in_specs=[vector] * 2,
        out_specs=(vector,) * 3,
        name="factor",
    )(gram, flat)


def summed(values):
    for axis in reversed(AXES):
        size = lax.axis_size(axis)
        if size & (size - 1):
            values = lax.psum(values, axis)
            continue
        step = 1
        while step < size:
            route = [(i, i ^ step) for i in range(size)]
            values = values + lax.ppermute(values, axis, route)
            step *= 2
    return values


def on_device(block_vectors, hamiltonian, pattern, owned_blocks, spectrum):
    block_count = pattern.shape[0]
    block_size = hamiltonian.shape[1]
    rows = block_vectors.shape[0]
    reach_dev = (BAND + block_count - 1) // block_count
    total = float(rows * lax.axis_size(AXES)) ** 0.5

    def extended(values):
        route = [d for d in range(reach_dev, -reach_dev - 1, -1)]
        return [shifted(values, d) if d else values for d in route]

    live = jnp.arange(rows, dtype=jnp.int32) < owned_blocks[0] * block_size
    first_vec = jnp.where(live[None, :], block_vectors.T, 0.0)
    second_vec = apply_matrix(
        pattern, owned_blocks, spectrum, extended(first_vec), None, hamiltonian
    )
    third_vec, local_gram = apply_matrix(
        pattern, owned_blocks, spectrum, extended(second_vec), first_vec, hamiltonian
    )
    basis, upper, spread = factor(summed(local_gram), third_vec, total)

    def second_pass(basis, upper):
        local = jnp.dot(
            basis, basis.T, precision=lax.Precision.HIGHEST, preferred_element_type=jnp.float32
        )
        again, upper_again, _ = factor(summed(local), basis, total)
        return again, jnp.dot(upper_again, upper, precision=lax.Precision.HIGHEST)

    basis, upper = lax.cond(
        spread[0, 0] <= 8.0 * basis.shape[0], lambda b, u: (b, u), second_pass, basis, upper
    )
    return basis.T, upper


def solution(mesh):
    placed = (
        P(AXES, None),
        P(AXES, None, None),
        P(AXES, None),
        P(AXES),
        P(),
    )
    return jax.shard_map(
        on_device,
        mesh=mesh,
        in_specs=placed,
        out_specs=(P(AXES, None), P()),
        check_vma=False,
    )
```

time: 226 us -> 91.3 us (0.40)
  blocking collectives: 89.1 us -> 0 us
  local copies, waits for them, and re-layouts: 43.3 us -> 5.96 us
  other arithmetic: 32.9 us -> 1.57 us
  starting transfers between devices: 20.4 us -> 43.9 us
  Pallas kernels: 0 us -> 22.6 us
  matrix products: 21.5 us -> 0 us
    psum x2 -> x0, blocking collectives: 89.1 us -> none  [summed_gram(): return lax.psum(local_gram, ('grp', 'dev'))]
    another operation x10 -> x0, other arithmetic: 24.3 us -> none  [the longest x6 13.1 us: cholesky_step(): upper = jnp.linalg.cholesky(gram_total).T]
    ppermute x8 -> x13, starting transfers between devices: 20.4 us -> 43.9 us  [the longest x5 22 us: summed(): values = values + lax.ppermute(values, axis, route)]
    pallas_call x0 -> x3, Pallas kernels: none -> 22.6 us  [the longest x2 15.2 us: apply_matrix(): pl.pallas_call(functools.partial(apply_kernel, first_apply, reach_dev), o...]
    dot_general x5 -> x0, matrix products: 20.2 us -> none  [the longest x2 17.4 us: apply_matrix(): jnp.einsum('gik,gkc->gic', hamiltonian, picked, precision=lax.Precision.H...]
    reshape x4 -> x0, local copies, waits for them, and re-layouts: 16.8 us -> none  [the longest x2 15.6 us: apply_matrix(): picked.reshape(block_count, neighbours * values.shape[1], values.shape[2])]
    select_n x2 -> x0, local copies, waits for them, and re-layouts: 16 us -> none  [apply_matrix(): picked = jnp.take(extended, local_index, axis=0)]
    gather x2 -> x0, local copies, waits for them, and re-layouts: 8.71 us -> none  [apply_matrix(): picked = jnp.take(extended, local_index, axis=0)]
  transfers between devices with their start and end apart: 8 -> 13, of which waited for: 4 -> 7; matrix products, arithmetic and copies ran while one was open for 1% -> 0% of each run, Pallas kernels for 0% -> 0%
where the time goes in v1:
time: 91.3 us; the launch traced here: 90.8 us
  starting transfers between devices  43.9 us (48%)
  Pallas kernels  22.6 us (25%)
  waiting for transfers between devices  14.8 us (16%)
  local copies, waits for them, and re-layouts  5.96 us (7%)
  between operations  2.1 us (2%)
  other arithmetic  1.57 us (2%)
    ppermute x5, starting transfers between devices, summed(): values = values + lax.ppermute(values, axis, route)  22 us
    ppermute x8, starting transfers between devices, shifted(): return lax.ppermute(block, AXES, route)  21.8 us
    pallas_call x2, Pallas kernels, apply_matrix(): pl.pallas_call(functools.partial(apply_kernel, first_apply, reach_dev), o...  15.2 us
    ppermute x5, waiting for transfers between devices, summed(): values = values + lax.ppermute(values, axis, route)  8.74 us
    pallas_call x1, Pallas kernels, factor(): pl.pallas_call(functools.partial(factor_kernel, total), out_shape=(jax.Sh...  7.35 us
    ppermute x8, waiting for transfers between devices, shifted(): return lax.ppermute(block, AXES, route)  6.01 us
    unnamed x12, local copies, waits for them, and re-layouts  4.78 us
  transfers between devices with their start and end apart: 13, of which 7 were waited for; matrix products, arithmetic and copies ran while one was open for 0% of the time, Pallas kernels for 0%

profile of v1, /device:TPU:0, one launch (start us, length us, event | category | flops | bytes accessed | tf_op | source)
XLA Modules:
  0.0 90.8 jit_solution(7457527100985532729)
XLA Ops:
  1.3 0.9 %select_bitcast_fusion.refs_2_.refs_5_ = f32[64,512]{1,0:T(8,128)S(1)} fusion(f32[512,64]{0,1:T(8,128)} %param.7, pred[512]{0:T(512)(128)(4,1)S(1)} %iota_compare_fusion), kind=kLoop, calls=%fused_computation | loop fusion | flops 32768 | bytes 262656 | tf_op jit(solution)/shard_map/jit(_where)/select_n | solution.py:210
  2.2 1.3 %collective-permute-start.8 = (f32[64,512]{1,0:T(8,128)S(1)}, f32[64,512]{1,0:T(8,128)S(1)}, u32[]{:S(2)}, u32[]{:S(2)}) collective-permute-start(f32[64,512]{1,0:T(8,128)S(1)} %select_bitcast_fusion.refs_2_.refs_5_), channel_id=1, source_target_pairs={{2,0},{3,1},{4,2},{5,3},{6,4},{7,5},{8,6},{9,7},{10,8},{11,9},{12,... | collective-permute-start | bytes 393224 | tf_op jit(solution)/shard_map/ppermute | solution.py:18
  3.5 1.3 %collective-permute-start.7 = (f32[64,512]{1,0:T(8,128)S(1)}, f32[64,512]{1,0:T(8,128)S(1)}, u32[]{:S(2)}, u32[]{:S(2)}) collective-permute-start(f32[64,512]{1,0:T(8,128)S(1)} %select_bitcast_fusion.refs_2_.refs_5_), channel_id=1, source_target_pairs={{1,0},{2,1},{3,2},{4,3},{5,4},{6,5},{7,6},{8,7},{9,8},{10,9},{11,1... | collective-permute-start | bytes 393224 | tf_op jit(solution)/shard_map/ppermute | solution.py:18
  4.8 3.0 %collective-permute-start.6 = (f32[64,512]{1,0:T(8,128)S(1)}, f32[64,512]{1,0:T(8,128)S(1)}, u32[]{:S(2)}, u32[]{:S(2)}) collective-permute-start(f32[64,512]{1,0:T(8,128)S(1)} %select_bitcast_fusion.refs_2_.refs_5_), channel_id=1, source_target_pairs={{0,1},{1,2},{2,3},{3,4},{4,5},{5,6},{6,7},{7,8},{8,9},{9,10},{10,1... | collective-permute-start | bytes 393224 | tf_op jit(solution)/shard_map/ppermute | solution.py:18
  7.9 5.6 %collective-permute-start.5 = (f32[64,512]{1,0:T(8,128)S(1)}, f32[64,512]{1,0:T(8,128)S(1)}, u32[]{:S(2)}, u32[]{:S(2)}) collective-permute-start(f32[64,512]{1,0:T(8,128)S(1)} %select_bitcast_fusion.refs_2_.refs_5_), channel_id=1, source_target_pairs={{0,2},{1,3},{2,4},{3,5},{4,6},{5,7},{6,8},{7,9},{8,10},{9,11},{10,... | collective-permute-start | bytes 393224 | tf_op jit(solution)/shard_map/ppermute | solution.py:18
  13.4 0.0 collective-permute-done.8.refs_4_
  13.4 0.0 collective-permute-done.7.refs_3_
  13.4 0.0 collective-permute-done.6.refs_1_
  13.5 3.2 %collective-permute-done.5.refs_0_ = f32[64,512]{1,0:T(8,128)S(1)} collective-permute-done((f32[64,512]{1,0:T(8,128)S(1)}, f32[64,512]{1,0:T(8,128)S(1)}, u32[]{:S(2)}, u32[]{:S(2)}) %collective-permute-start.5) | collective-permute-done | bytes 131104 | tf_op jit(solution)/shard_map/ppermute | solution.py:18
  16.7 0.0 copy-start
  16.7 2.2 %copy-done = f32[8,64,2048]{2,1,0:T(8,128)S(1)} copy-done((f32[8,64,2048]{2,1,0:T(8,128)S(1)}, f32[8,64,2048]{2,1,0:T(8,128)}, u32[]{:S(2)}) %copy-start) | copy-done | bytes 4194328
  18.9 0.0 copy-start.3
  18.9 0.7 copy-done.3
  19.6 0.0 copy-start.4
  19.6 0.7 copy-done.4
  20.2 0.0 copy-start.1
  20.2 7.4 %apply_first.1.refs_2_ = f32[64,512]{1,0:T(8,128)S(1)} custom-call(s32[8,32]{1,0:T(8,128)S(1)} %copy-done.3, s32[1]{0:T(128)S(6)} %copy.13.owned_ref, f32[2]{0:T(128)S(1)} %copy-done.4, f32[64,512]{1,0:T(8,128)S(1)} %collective-permute-done.5.refs_0_, f32[64,512]{1,0:T(8,128)S(1)} %collective-permute-done.6.refs_1_, ...), custom_call_target="tpu_custom_call" | custom-call | tf_op jit(solution)/shard_map/apply_first/pallas_call | solution.py:115
  27.6 1.3 %collective-permute-start.12 = (f32[64,512]{1,0:T(8,128)S(1)}, f32[64,512]{1,0:T(8,128)S(1)}, u32[]{:S(2)}, u32[]{:S(2)}) collective-permute-start(f32[64,512]{1,0:T(8,128)S(1)} %apply_first.1.refs_2_), channel_id=1, source_target_pairs={{2,0},{3,1},{4,2},{5,3},{6,4},{7,5},{8,6},{9,7},{10,8},{11,9},{12,... | collective-permute-start | bytes 393224 | tf_op jit(solution)/shard_map/ppermute | solution.py:18
  28.9 1.3 %collective-permute-start.11 = (f32[64,512]{1,0:T(8,128)S(1)}, f32[64,512]{1,0:T(8,128)S(1)}, u32[]{:S(2)}, u32[]{:S(2)}) collective-permute-start(f32[64,512]{1,0:T(8,128)S(1)} %apply_first.1.refs_2_), channel_id=1, source_target_pairs={{1,0},{2,1},{3,2},{4,3},{5,4},{6,5},{7,6},{8,7},{9,8},{10,9},{11,1... | collective-permute-start | bytes 393224 | tf_op jit(solution)/shard_map/ppermute | solution.py:18
  30.2 3.3 %collective-permute-start.10 = (f32[64,512]{1,0:T(8,128)S(1)}, f32[64,512]{1,0:T(8,128)S(1)}, u32[]{:S(2)}, u32[]{:S(2)}) collective-permute-start(f32[64,512]{1,0:T(8,128)S(1)} %apply_first.1.refs_2_), channel_id=1, source_target_pairs={{0,1},{1,2},{2,3},{3,4},{4,5},{5,6},{6,7},{7,8},{8,9},{9,10},{10,1... | collective-permute-start | bytes 393224 | tf_op jit(solution)/shard_map/ppermute | solution.py:18
  33.5 4.8 %collective-permute-start.9 = (f32[64,512]{1,0:T(8,128)S(1)}, f32[64,512]{1,0:T(8,128)S(1)}, u32[]{:S(2)}, u32[]{:S(2)}) collective-permute-start(f32[64,512]{1,0:T(8,128)S(1)} %apply_first.1.refs_2_), channel_id=1, source_target_pairs={{0,2},{1,3},{2,4},{3,5},{4,6},{5,7},{6,8},{7,9},{8,10},{9,11},{10,... | collective-permute-start | bytes 393224 | tf_op jit(solution)/shard_map/ppermute | solution.py:18
  38.3 0.0 collective-permute-done.12.refs_4_
  38.3 0.0 collective-permute-done.11.refs_3_
  38.3 0.0 collective-permute-done.10.refs_1_
  38.3 2.8 %collective-permute-done.9.refs_0_ = f32[64,512]{1,0:T(8,128)S(1)} collective-permute-done((f32[64,512]{1,0:T(8,128)S(1)}, f32[64,512]{1,0:T(8,128)S(1)}, u32[]{:S(2)}, u32[]{:S(2)}) %collective-permute-start.9) | collective-permute-done | bytes 131104 | tf_op jit(solution)/shard_map/ppermute | solution.py:18
  41.1 0.0 copy-done.1
  41.1 7.8 %apply_second.1 = (f32[64,512]{1,0:T(8,128)S(1)}, f32[64,64]{1,0:T(8,128)S(1)}) custom-call(s32[8,32]{1,0:T(8,128)S(1)} %copy-done.3, s32[1]{0:T(128)S(6)} %copy.13.owned_ref, f32[2]{0:T(128)S(1)} %copy-done.4, f32[64,512]{1,0:T(8,128)S(1)} %collective-permute-done.9.refs_0_, f32[64,512]{1,0:T(8,128)S(1)} %collective-permute-done.10.refs_1_, ...), custom_call_target="tpu_custom_call" | custom-call | tf_op jit(solution)/shard_map/apply_second/pallas_call | solution.py:115
  48.9 0.0 copy-start.2
  48.9 0.6 copy-done.2
  49.6 1.2 %collective-permute-start.13 = (f32[64,64]{1,0:T(8,128)S(1)}, f32[64,64]{1,0:T(8,128)S(1)}, u32[]{:S(2)}, u32[]{:S(2)}) collective-permute-start(f32[64,64]{1,0:T(8,128)S(1)} %get-tuple-element.21), channel_id=1, source_target_pairs={{0,1},{1,0},{2,3},{3,2},{4,5},{5,4},{6,7},{7,6},{8,9},{9,8},{10,11... | collective-permute-start | bytes 49160 | tf_op jit(solution)/shard_map/ppermute | solution.py:193
  50.7 0.9 collective-permute-done.13
  51.6 3.1 %collective-permute-start.14 = (f32[64,64]{1,0:T(8,128)S(1)}, f32[64,64]{1,0:T(8,128)S(1)}, u32[]{:S(2)}, u32[]{:S(2)}) collective-permute-start(f32[64,64]{1,0:T(8,128)S(1)} %add.30), channel_id=1, source_target_pairs={{0,2},{1,3},{2,0},{3,1},{4,6},{5,7},{6,4},{7,5},{8,10},{9,11},{10,... | collective-permute-start | bytes 49160 | tf_op jit(solution)/shard_map/ppermute | solution.py:193
  54.7 1.9 %collective-permute-done.14 = f32[64,64]{1,0:T(8,128)S(1)} collective-permute-done((f32[64,64]{1,0:T(8,128)S(1)}, f32[64,64]{1,0:T(8,128)S(1)}, u32[]{:S(2)}, u32[]{:S(2)}) %collective-permute-start.14) | collective-permute-done | bytes 16416 | tf_op jit(solution)/shard_map/ppermute | solution.py:193
  56.6 7.3 %collective-permute-start.15 = (f32[64,64]{1,0:T(8,128)S(1)}, f32[64,64]{1,0:T(8,128)S(1)}, u32[]{:S(2)}, u32[]{:S(2)}) collective-permute-start(f32[64,64]{1,0:T(8,128)S(1)} %add.31), channel_id=1, source_target_pairs={{0,4},{1,5},{2,6},{3,7},{4,0},{5,1},{6,2},{7,3},{8,12},{9,13},{10,... | collective-permute-start | bytes 49160 | tf_op jit(solution)/shard_map/ppermute | solution.py:193
  63.9 2.2 %collective-permute-done.15 = f32[64,64]{1,0:T(8,128)S(1)} collective-permute-done((f32[64,64]{1,0:T(8,128)S(1)}, f32[64,64]{1,0:T(8,128)S(1)}, u32[]{:S(2)}, u32[]{:S(2)}) %collective-permute-start.15) | collective-permute-done | bytes 16416 | tf_op jit(solution)/shard_map/ppermute | solution.py:193
  66.1 5.7 %collective-permute-start.16 = (f32[64,64]{1,0:T(8,128)S(1)}, f32[64,64]{1,0:T(8,128)S(1)}, u32[]{:S(2)}, u32[]{:S(2)}) collective-permute-start(f32[64,64]{1,0:T(8,128)S(1)} %add.32), channel_id=1, source_target_pairs={{0,8},{8,0},{16,24},{24,16},{1,9},{9,1},{17,25},{25,17},{2,10},{10... | collective-permute-start | bytes 49160 | tf_op jit(solution)/shard_map/ppermute | solution.py:193
  71.8 1.9 %collective-permute-done.16 = f32[64,64]{1,0:T(8,128)S(1)} collective-permute-done((f32[64,64]{1,0:T(8,128)S(1)}, f32[64,64]{1,0:T(8,128)S(1)}, u32[]{:S(2)}, u32[]{:S(2)}) %collective-permute-start.16) | collective-permute-done | bytes 16416 | tf_op jit(solution)/shard_map/ppermute | solution.py:193
  73.7 4.7 %collective-permute-start.17 = (f32[64,64]{1,0:T(8,128)S(1)}, f32[64,64]{1,0:T(8,128)S(1)}, u32[]{:S(2)}, u32[]{:S(2)}) collective-permute-start(f32[64,64]{1,0:T(8,128)S(1)} %add.33), channel_id=1, source_target_pairs={{0,16},{8,24},{16,0},{24,8},{1,17},{9,25},{17,1},{25,9},{2,18},{10... | collective-permute-start | bytes 49160 | tf_op jit(solution)/shard_map/ppermute | solution.py:193
  78.5 1.9 %collective-permute-done.17 = f32[64,64]{1,0:T(8,128)S(1)} collective-permute-done((f32[64,64]{1,0:T(8,128)S(1)}, f32[64,64]{1,0:T(8,128)S(1)}, u32[]{:S(2)}, u32[]{:S(2)}) %collective-permute-start.17) | collective-permute-done | bytes 16416 | tf_op jit(solution)/shard_map/ppermute | solution.py:193
  80.4 0.6 add.34.gram_ref
  81.0 7.3 %factor.3 = (f32[64,512]{1,0:T(8,128)}, f32[64,64]{1,0:T(8,128)S(1)}, f32[8,128]{1,0:T(8,128)}) custom-call(f32[64,64]{1,0:T(8,128)} %add.34.gram_ref, f32[64,512]{1,0:T(8,128)} %copy-done.2), custom_call_target="tpu_custom_call" | custom-call | tf_op jit(solution)/shard_map/factor/pallas_call | solution.py:171
  88.3 1.2 %slice.3 = f32[1,1]{1,0:T(1,128)} slice(f32[8,128]{1,0:T(8,128)} %get-tuple-element.23), slice={[0:1], [0:1]} | slice | bytes 8 | tf_op jit(solution)/shard_map/slice | solution.py:227
  90.2 0.0 copy-start.6
  90.2 0.6 copy-done.6
  (6 shorter events, 0.0 us)
Async XLA Ops:
  2.2 11.2 %collective-permute-start.8 = (f32[64,512]{1,0:T(8,128)S(1)}, f32[64,512]{1,0:T(8,128)S(1)}, u32[]{:S(2)}, u32[]{:S(2)}) collective-permute-start(f32[64,512]{1,0:T(8,128)S(1)} %select_bitcast_fusion.refs_2_.refs_5_), channel_id=1, source_target_pairs={{2,0},{3,1},{4,2},{5,3},{6,4},{7,5},{8,6},{9,7},{10,8},{11,9},{12,... | collective-permute-start | bytes 393224 | tf_op jit(solution)/shard_map/ppermute | solution.py:18
  3.5 9.9 %collective-permute-start.7 = (f32[64,512]{1,0:T(8,128)S(1)}, f32[64,512]{1,0:T(8,128)S(1)}, u32[]{:S(2)}, u32[]{:S(2)}) collective-permute-start(f32[64,512]{1,0:T(8,128)S(1)} %select_bitcast_fusion.refs_2_.refs_5_), channel_id=1, source_target_pairs={{1,0},{2,1},{3,2},{4,3},{5,4},{6,5},{7,6},{8,7},{9,8},{10,9},{11,1... | collective-permute-start | bytes 393224 | tf_op jit(solution)/shard_map/ppermute | solution.py:18
  4.8 8.6 %collective-permute-start.6 = (f32[64,512]{1,0:T(8,128)S(1)}, f32[64,512]{1,0:T(8,128)S(1)}, u32[]{:S(2)}, u32[]{:S(2)}) collective-permute-start(f32[64,512]{1,0:T(8,128)S(1)} %select_bitcast_fusion.refs_2_.refs_5_), channel_id=1, source_target_pairs={{0,1},{1,2},{2,3},{3,4},{4,5},{5,6},{6,7},{7,8},{8,9},{9,10},{10,1... | collective-permute-start | bytes 393224 | tf_op jit(solution)/shard_map/ppermute | solution.py:18
  7.9 8.8 %collective-permute-start.5 = (f32[64,512]{1,0:T(8,128)S(1)}, f32[64,512]{1,0:T(8,128)S(1)}, u32[]{:S(2)}, u32[]{:S(2)}) collective-permute-start(f32[64,512]{1,0:T(8,128)S(1)} %select_bitcast_fusion.refs_2_.refs_5_), channel_id=1, source_target_pairs={{0,2},{1,3},{2,4},{3,5},{4,6},{5,7},{6,8},{7,9},{8,10},{9,11},{10,... | collective-permute-start | bytes 393224 | tf_op jit(solution)/shard_map/ppermute | solution.py:18
  16.7 2.2 %copy-start = (f32[8,64,2048]{2,1,0:T(8,128)S(1)}, f32[8,64,2048]{2,1,0:T(8,128)}, u32[]{:S(2)}) copy-start(f32[8,64,2048]{2,1,0:T(8,128)} %refs_6_.1) | copy-start | bytes 12582916
  18.9 0.7 copy-start.3
  19.6 0.7 copy-start.4
  20.2 20.9 %copy-start.1 = (f32[8,64,2048]{2,1,0:T(8,128)S(1)}, f32[8,64,2048]{2,1,0:T(8,128)}, u32[]{:S(2)}) copy-start(f32[8,64,2048]{2,1,0:T(8,128)} %refs_6_.1) | copy-start | bytes 12582916
  27.6 10.7 %collective-permute-start.12 = (f32[64,512]{1,0:T(8,128)S(1)}, f32[64,512]{1,0:T(8,128)S(1)}, u32[]{:S(2)}, u32[]{:S(2)}) collective-permute-start(f32[64,512]{1,0:T(8,128)S(1)} %apply_first.1.refs_2_), channel_id=1, source_target_pairs={{2,0},{3,1},{4,2},{5,3},{6,4},{7,5},{8,6},{9,7},{10,8},{11,9},{12,... | collective-permute-start | bytes 393224 | tf_op jit(solution)/shard_map/ppermute | solution.py:18
  28.9 9.4 %collective-permute-start.11 = (f32[64,512]{1,0:T(8,128)S(1)}, f32[64,512]{1,0:T(8,128)S(1)}, u32[]{:S(2)}, u32[]{:S(2)}) collective-permute-start(f32[64,512]{1,0:T(8,128)S(1)} %apply_first.1.refs_2_), channel_id=1, source_target_pairs={{1,0},{2,1},{3,2},{4,3},{5,4},{6,5},{7,6},{8,7},{9,8},{10,9},{11,1... | collective-permute-start | bytes 393224 | tf_op jit(solution)/shard_map/ppermute | solution.py:18
  30.2 8.1 %collective-permute-start.10 = (f32[64,512]{1,0:T(8,128)S(1)}, f32[64,512]{1,0:T(8,128)S(1)}, u32[]{:S(2)}, u32[]{:S(2)}) collective-permute-start(f32[64,512]{1,0:T(8,128)S(1)} %apply_first.1.refs_2_), channel_id=1, source_target_pairs={{0,1},{1,2},{2,3},{3,4},{4,5},{5,6},{6,7},{7,8},{8,9},{9,10},{10,1... | collective-permute-start | bytes 393224 | tf_op jit(solution)/shard_map/ppermute | solution.py:18
  33.5 7.6 %collective-permute-start.9 = (f32[64,512]{1,0:T(8,128)S(1)}, f32[64,512]{1,0:T(8,128)S(1)}, u32[]{:S(2)}, u32[]{:S(2)}) collective-permute-start(f32[64,512]{1,0:T(8,128)S(1)} %apply_first.1.refs_2_), channel_id=1, source_target_pairs={{0,2},{1,3},{2,4},{3,5},{4,6},{5,7},{6,8},{7,9},{8,10},{9,11},{10,... | collective-permute-start | bytes 393224 | tf_op jit(solution)/shard_map/ppermute | solution.py:18
  48.9 0.7 copy-start.2
  49.6 2.0 %collective-permute-start.13 = (f32[64,64]{1,0:T(8,128)S(1)}, f32[64,64]{1,0:T(8,128)S(1)}, u32[]{:S(2)}, u32[]{:S(2)}) collective-permute-start(f32[64,64]{1,0:T(8,128)S(1)} %get-tuple-element.21), channel_id=1, source_target_pairs={{0,1},{1,0},{2,3},{3,2},{4,5},{5,4},{6,7},{7,6},{8,9},{9,8},{10,11... | collective-permute-start | bytes 49160 | tf_op jit(solution)/shard_map/ppermute | solution.py:193
  51.6 5.0 %collective-permute-start.14 = (f32[64,64]{1,0:T(8,128)S(1)}, f32[64,64]{1,0:T(8,128)S(1)}, u32[]{:S(2)}, u32[]{:S(2)}) collective-permute-start(f32[64,64]{1,0:T(8,128)S(1)} %add.30), channel_id=1, source_target_pairs={{0,2},{1,3},{2,0},{3,1},{4,6},{5,7},{6,4},{7,5},{8,10},{9,11},{10,... | collective-permute-start | bytes 49160 | tf_op jit(solution)/shard_map/ppermute | solution.py:193
  56.6 9.5 %collective-permute-start.15 = (f32[64,64]{1,0:T(8,128)S(1)}, f32[64,64]{1,0:T(8,128)S(1)}, u32[]{:S(2)}, u32[]{:S(2)}) collective-permute-start(f32[64,64]{1,0:T(8,128)S(1)} %add.31), channel_id=1, source_target_pairs={{0,4},{1,5},{2,6},{3,7},{4,0},{5,1},{6,2},{7,3},{8,12},{9,13},{10,... | collective-permute-start | bytes 49160 | tf_op jit(solution)/shard_map/ppermute | solution.py:193
  66.1 7.6 %collective-permute-start.16 = (f32[64,64]{1,0:T(8,128)S(1)}, f32[64,64]{1,0:T(8,128)S(1)}, u32[]{:S(2)}, u32[]{:S(2)}) collective-permute-start(f32[64,64]{1,0:T(8,128)S(1)} %add.32), channel_id=1, source_target_pairs={{0,8},{8,0},{16,24},{24,16},{1,9},{9,1},{17,25},{25,17},{2,10},{10... | collective-permute-start | bytes 49160 | tf_op jit(solution)/shard_map/ppermute | solution.py:193
  73.7 6.6 %collective-permute-start.17 = (f32[64,64]{1,0:T(8,128)S(1)}, f32[64,64]{1,0:T(8,128)S(1)}, u32[]{:S(2)}, u32[]{:S(2)}) collective-permute-start(f32[64,64]{1,0:T(8,128)S(1)} %add.33), channel_id=1, source_target_pairs={{0,16},{8,24},{16,0},{24,8},{1,17},{9,25},{17,1},{25,9},{2,18},{10... | collective-permute-start | bytes 49160 | tf_op jit(solution)/shard_map/ppermute | solution.py:193
  90.2 0.6 copy-start.6
